TPU v7x, 32 devices: a whole 2x2x4 slice. The times are simulated.
32 devices in a mesh: groups: 2 (over y), block: 4 (over x, core), slab: 4 (over z).
Axes of the slice: x: 2, y: 2, z: 4, core: 2. Of those that a mesh axis runs over, the one named last changes fastest.
Arguments:
- point_coords: float32 [3, 131072], P(None, ('groups', 'block', 'slab')), parts along dimension 1, may hold values from -1 to 1
- point_normals: float32 [3, 131072], P(None, ('groups', 'block', 'slab')), parts along dimension 1, may hold values from -4 to 4
- strengths: float32 [2, 131072], P(None, ('groups', 'block', 'slab')), parts along dimension 1, may hold values from -1.2 to 1.2
- point_counts: int32 [32, 256], P(('groups', 'block', 'slab')), parts along dimension 0, may hold values from 1 to 16, 2560 in all within a row
- leaf_list: int32 [8192, 316], P(('groups', 'block', 'slab')), parts along dimension 0, may hold values from 0 to 1, as said below
- parent_list: int32 [1024, 316], P(('groups', 'block', 'slab')), parts along dimension 0, may hold values from 0 to 1, as said below
- summit_list: int32 [128, 316], P(('groups', 'block', 'slab')), parts along dimension 0, may hold values from 0 to 1, as said below
- translations: float32 [316, 32, 32], replicated, may hold values from -0.078125 to 0.078125
- compress: float32 [216, 32], replicated, may hold values from -0.4375 to 0.4375
- expand: float32 [216, 32], replicated, may hold values from -1 to 1
Outputs:
- potential: float32 [2, 131072], P(None, ('groups', 'block', 'slab')), parts along dimension 1
There are 2 independent parts, one for each index of `groups`. A program takes and returns all parts, laid end to end along the dimension named above; an argument that names none is the same for every part. Nothing has to cross between parts.
Inputs may be any that keep to these rules, and one draw needn't show every extreme that they name: `leaf_list`: 1 where the box at that offset is in the target box's far-field list of the level; a box is listed only where its parent neighbours the target's parent. `parent_list`: as leaf_list, one level up. `summit_list`: as leaf_list, two levels up.
All inputs are finite; a program needn't handle non-finite values.
Results may differ from a plain program's by a relative error of at most 0.0003.
Values sent between devices are 32-bit elements; how exact they have to be, the bound alone decides.
A program may use at most 128 MiB of HBM per device.

v0:
```python
import jax
import jax.numpy as jnp
import numpy as np
from jax import lax
from jax.sharding import PartitionSpec as P

ORDER = 6
BX = 8
BZ = 8


highest = lax.Precision.HIGHEST
parent_scale = 0.5
summit_scale = 0.25


def with_halo(cells, sides, width):
    for axis, dim in sides:
        count = lax.axis_size(axis)
        ends = count - 1
        head = lax.slice_in_dim(cells, 0, width, axis=dim)
        tail = lax.slice_in_dim(cells, cells.shape[dim] - width, cells.shape[dim], axis=dim)
        cells = jnp.concatenate(
            [
                lax.ppermute(tail, axis, [(i, (i + 1) % count) for i in range(ends)]),
                cells,
                lax.ppermute(head, axis, [((i + 1) % count, i) for i in range(ends)]),
            ],
            axis=dim,
        )
    return cells


def offset_list():
    listing = []
    for shift_x in range(-3, 4):
        for shift_y in range(-3, 4):
            for shift_z in range(-3, 4):
                if max(abs(shift_x), abs(shift_y), abs(shift_z)) > 1:
                    listing.append((shift_x, shift_y, shift_z))
    return listing


def chebyshev_terms(values, degree_count):
    firsts = [jnp.ones_like(values), values]
    slopes = [jnp.zeros_like(values), jnp.ones_like(values)]
    for degree in range(2, degree_count):
        firsts.append(2.0 * values * firsts[-1] - firsts[-2])
        slopes.append(2.0 * firsts[-2] + 2.0 * values * slopes[-1] - slopes[-2])
    return (jnp.stack(firsts[:degree_count]), jnp.stack(slopes[:degree_count]))


def basis_coefficients(node_order):
    angles = (2.0 * np.arange(node_order) + 1.0) * np.pi / (2.0 * node_order)
    degrees = np.arange(node_order)
    weights = np.where(degrees == 0, 1.0, 2.0) / node_order
    basis_table = np.cos(angles[:, None] * degrees[None, :]) * weights[None, :]
    return (jnp.asarray(basis_table, jnp.float32), np.cos(angles))


def child_operators(node_order):
    basis_table, node_points = basis_coefficients(node_order)
    inside = jnp.asarray(
        np.stack([(node_points - 1.0) / 2.0, (node_points + 1.0) / 2.0]), jnp.float32
    )
    values, slopes = chebyshev_terms(inside, node_order)
    return jnp.einsum("ik,ksa->sia", basis_table, values, precision=highest)


def multipole_block(coords, normals, charges, basis_table, node_order):
    values, slopes = chebyshev_terms(coords, node_order)
    interp = jnp.einsum("ak,kdls->adls", basis_table, values, precision=highest)
    derivative = jnp.einsum("ak,kdls->adls", basis_table, slopes, precision=highest)
    along_x = jnp.einsum(
        "als,bls,cls,rls->lrabc",
        derivative[:, 0],
        interp[:, 1],
        interp[:, 2],
        charges * normals[0][None],
        precision=highest,
    )
    along_y = jnp.einsum(
        "als,bls,cls,rls->lrabc",
        interp[:, 0],
        derivative[:, 1],
        interp[:, 2],
        charges * normals[1][None],
        precision=highest,
    )
    along_z = jnp.einsum(
        "als,bls,cls,rls->lrabc",
        interp[:, 0],
        interp[:, 1],
        derivative[:, 2],
        charges * normals[2][None],
        precision=highest,
    )
    summed = along_x + along_y + along_z
    return (summed.reshape(summed.shape[0], summed.shape[1], node_order**3), interp)


def potential_block(interp, field, node_order):
    grouped = field.reshape(field.shape[0], field.shape[1], node_order, node_order, node_order)
    return jnp.einsum(
        "lrabc,als,bls,cls->rls",
        grouped,
        interp[:, 0],
        interp[:, 1],
        interp[:, 2],
        precision=highest,
    )


def merge_children(poles, children, node_order):
    extent_x, extent_z, extent_y, rhs_count, node_count = poles.shape
    grouped = poles.reshape(
        extent_x // 2,
        2,
        extent_z // 2,
        2,
        extent_y // 2,
        2,
        rhs_count,
        node_order,
        node_order,
        node_order,
    )
    merged = jnp.einsum(
        "xpzqyvrabc,pia,vjb,qlc->xzyrijl", grouped, children, children, children, precision=highest
    )
    return merged.reshape(extent_x // 2, extent_z // 2, extent_y // 2, rhs_count, node_count)


def spread_children(field, children, node_order):
    extent_x, extent_z, extent_y, rhs_count, node_count = field.shape
    grouped = field.reshape(
        extent_x, extent_z, extent_y, rhs_count, node_order, node_order, node_order
    )
    spread = jnp.einsum(
        "xzyrijl,pia,vjb,qlc->xpzqyvrabc", grouped, children, children, children, precision=highest
    )
    return spread.reshape(2 * extent_x, 2 * extent_z, 2 * extent_y, rhs_count, node_count)


def compress_level(poles, compress):
    coefficient = jnp.einsum("xzyrn,nk->xzyrk", poles, compress, precision=highest)
    return coefficient.reshape(coefficient.shape[0], coefficient.shape[1], -1)


def expand_level(local_part, expand):
    return jnp.einsum("xzyrk,nk->xzyrn", local_part, expand, precision=highest)


def widen_y(extended, extent_y, columns):
    first_size, second_size = (extended.shape[0], extended.shape[1])
    grouped = extended.reshape(first_size, second_size, extent_y, columns)
    grouped = jnp.pad(grouped, ((0, 0), (0, 0), (3, 3), (0, 0)))
    return grouped.reshape(first_size, second_size, (extent_y + 6) * columns)


def translate_level(extended, listing, translations, factor, extents):
    span_x, span_z, span_y, rhs_count, rank_size = extents
    offsets = offset_list()
    columns = rhs_count * rank_size
    selectors = jnp.moveaxis(listing.reshape(span_x, span_z, span_y, len(offsets)), 3, 1).astype(
        jnp.float32
    )

    def one_plane(inputs):
        position, mask_plane = inputs
        window = lax.dynamic_slice_in_dim(extended, position, 7, 0)
        total = jnp.zeros((span_z, span_y, rhs_count, rank_size), jnp.float32)
        for shift_group in range(-3, 4):
            chosen = [index for index in range(len(offsets)) if offsets[index][0] == shift_group]
            first, last = (chosen[0], chosen[-1] + 1)
            pieces = [
                window[
                    3 + offsets[index][0],
                    3 + offsets[index][2] : 3 + offsets[index][2] + span_z,
                    (3 + offsets[index][1]) * columns : (3 + offsets[index][1] + span_y) * columns,
                ]
                for index in chosen
            ]
            stacked = jnp.stack(pieces).reshape(len(chosen), span_z, span_y, rhs_count, rank_size)
            stacked = stacked * mask_plane[first:last, :, :, None, None]
            total = total + jnp.einsum(
                "ozyrk,oik->zyri", stacked, translations[first:last], precision=highest
            )
        return total

    result = lax.map(one_plane, (jnp.arange(span_x, dtype=jnp.int32), selectors))
    return factor * result


def grid_window(gathered, extent_x, extent_z):
    blocks = lax.axis_size("block")
    slabs = lax.axis_size("slab")
    columns = gathered.shape[-1]
    grid = gathered.reshape(blocks, slabs, extent_x, extent_z, columns)
    grid = jnp.transpose(grid, (0, 2, 1, 3, 4)).reshape(
        blocks * extent_x, slabs * extent_z, columns
    )
    padded = jnp.pad(grid, ((3, 3), (3, 3), (0, 0)))
    start_x = lax.axis_index("block") * extent_x
    start_z = lax.axis_index("slab") * extent_z
    return lax.dynamic_slice(padded, (start_x, start_z, 0), (extent_x + 6, extent_z + 6, columns))


def body(
    point_coords,
    point_normals,
    strengths,
    point_counts,
    leaf_list,
    parent_list,
    summit_list,
    translations,
    compress,
    expand,
):
    node_order = ORDER
    basis_table, node_points = basis_coefficients(node_order)
    children = child_operators(node_order)
    rhs_count = strengths.shape[0]
    rank_size = compress.shape[1]
    columns = rhs_count * rank_size
    leaf_count = leaf_list.shape[0]
    extent_x = BX
    extent_z = BZ
    extent_y = leaf_count // (extent_x * extent_z)
    slots = point_coords.shape[1] // leaf_count
    filled = (
        jnp.arange(slots, dtype=jnp.int32)[None, :] < point_counts.reshape(leaf_count, 1)
    ).astype(jnp.float32)
    charges = strengths.reshape(rhs_count, leaf_count, slots) * filled[None]

    def by_plane(values):
        return jnp.moveaxis(
            values.reshape(values.shape[0], extent_x, extent_z * extent_y, slots), 1, 0
        )

    def plane_poles(pieces):
        return multipole_block(pieces[0], pieces[1], pieces[2], basis_table, node_order)

    poles, interp = lax.map(
        plane_poles, (by_plane(point_coords), by_plane(point_normals), by_plane(charges))
    )
    leaf_poles = poles.reshape(extent_x, extent_z, extent_y, rhs_count, -1)
    parent_poles = merge_children(leaf_poles, children, node_order)
    summit_poles = merge_children(parent_poles, children, node_order)
    leaf_coef = compress_level(leaf_poles, compress)
    parent_coef = compress_level(parent_poles, compress)
    summit_coef = compress_level(summit_poles, compress)
    leaf_extents = (extent_x, extent_z, extent_y, rhs_count, rank_size)
    leaf_ext = with_halo(leaf_coef, (("block", 0), ("slab", 1)), 3)
    leaf_local = translate_level(
        widen_y(leaf_ext, extent_y, columns), leaf_list, translations, 1.0, leaf_extents
    )
    parent_ext = with_halo(parent_coef, (("block", 0), ("slab", 1)), 3)
    summit_all = lax.all_gather(summit_coef[None], ("block", "slab"), axis=0, tiled=True)
    summit_ext = grid_window(summit_all, extent_x // 4, extent_z // 4)
    parent_extents = (extent_x // 2, extent_z // 2, extent_y // 2, rhs_count, rank_size)
    summit_extents = (extent_x // 4, extent_z // 4, extent_y // 4, rhs_count, rank_size)
    parent_local = translate_level(
        widen_y(parent_ext, extent_y // 2, columns),
        parent_list,
        translations,
        parent_scale,
        parent_extents,
    )
    summit_local = translate_level(
        widen_y(summit_ext, extent_y // 4, columns),
        summit_list,
        translations,
        summit_scale,
        summit_extents,
    )
    summit_field = expand_level(summit_local, expand)
    parent_field = expand_level(parent_local, expand) + spread_children(
        summit_field, children, node_order
    )
    leaf_field = expand_level(leaf_local, expand) + spread_children(
        parent_field, children, node_order
    )

    def plane_potential(pieces):
        return potential_block(pieces[0], pieces[1], node_order)

    result = lax.map(
        plane_potential, (interp, leaf_field.reshape(extent_x, extent_z * extent_y, rhs_count, -1))
    )
    return jnp.moveaxis(result, 0, 1).reshape(rhs_count, -1)


def solution(mesh):
    return jax.shard_map(
        body,
        mesh=mesh,
        in_specs=(
            P(None, ("groups", "block", "slab")),
            P(None, ("groups", "block", "slab")),
            P(None, ("groups", "block", "slab")),
            P(("groups", "block", "slab"), None),
            P(("groups", "block", "slab"), None),
            P(("groups", "block", "slab"), None),
            P(("groups", "block", "slab"), None),
            P(),
            P(),
            P(),
        ),
        out_specs=P(None, ("groups", "block", "slab")),
        check_vma=False,
    )
```

profile of v0, /device:TPU:0, one launch (start us, length us, event | category | flops | bytes accessed | tf_op | source)
XLA Modules:
  0.0 1745.2 jit_solution(4138864060988602720)
XLA Ops:
  6.6 404.5 %while.60 = (s32[]{:T(128)}, f32[8,32,2,216]{1,2,3,0:T(2,128)}, f32[8,6,3,32,16]{3,4,2,1,0:T(8,128)}, f32[8,2,32,16]{3,2,0,1:T(8,128)}, f32[8,3,32,16]{3,2,0,1:T...) while((s32[]{:T(128)}, f32[8,32,2,216]{1,2,3,0:T(2,128)}, ...), condition=%wide.region_1.2_spmd.clone, body=%wide.region_0.1_spmd.sunk.clone.sunk | while | flops 9498626 | bytes 2256369 | solution.py:245
  15.8 10.5 fusion.368
  27.8 11.5 fusion.367
  40.9 12.6 add_bitcast_fusion.2
  66.3 10.5 fusion.368
  78.3 11.5 fusion.367
  91.4 12.6 add_bitcast_fusion.2
  116.8 10.5 fusion.368
  128.8 11.5 fusion.367
  141.9 12.6 add_bitcast_fusion.2
  167.3 10.5 fusion.368
  179.3 11.5 fusion.367
  192.4 12.6 add_bitcast_fusion.2
  217.9 10.5 fusion.368
  229.8 11.5 fusion.367
  242.9 12.6 add_bitcast_fusion.2
  268.4 10.5 fusion.368
  280.4 11.5 fusion.367
  293.5 12.6 add_bitcast_fusion.2
  318.9 10.5 fusion.368
  330.9 11.5 fusion.367
  344.0 12.6 add_bitcast_fusion.2
  369.4 10.5 fusion.368
  381.4 11.5 fusion.367
  394.5 12.6 add_bitcast_fusion.2
  422.5 7.2 reshape_reshape.4
  429.7 20.4 %fusion.160 = f32[6,4,4,2,2,2,2,6,6]{8,0,7,6,5,4,3,2,1:T(8,128)S(1)} fusion(f32[2,6,6,1,1,1,1,1,1,1]{2,1,0,9,8,7,6,5,4,3:T(8,128)S(1)} %copy-done.24, f32[4,2,4,2,2,2,2,6,6,6]{9,8,7,5,4,3,2,6,1,0:T(8,128)} %reshape_reshape.4), kind=kOutput, calls=%fused_computation.1051 | convolution fusion | flops 7962624 | bytes 663840 | tf_op jit(solution)/shard_map/xpzqyvrabc,pia,vjb,qlc->xzyrijl/dot_general | solution.py:128
  450.2 6.5 fusion.151
  461.7 5.1 collective-permute-start.4
  475.4 34.0 %all_gather.3 = f32[16,2,2,64]{3,2,1,0:T(2,128)S(1)} all-gather(f32[1,2,2,64]{3,2,1,0:T(2,128)S(1)} %broadcast_in_dim_reshape.3), channel_id=1, replica_groups=mesh['groups'=2,'block'=4,'slab'=4] {'block','slab'}, dimensions={0}, use_global_device_ids=true | all-gather | bytes 17408 | tf_op jit(solution)/shard_map/all_gather | solution.py:260
  512.1 100.0 %while.58 = (s32[]{:T(128)}, f32[2,2,1,2,32]{4,3,1,2,0:T(2,128)}, s32[2]{0:T(128)}, f32[8,8,448]{0,2,1:T(8,128)S(1)}, f32[2,316,2,1]{1,2,3,0:T(2,128)S(1)}, /*in...) while((s32[]{:T(128)}, f32[2,2,1,2,32]{4,3,1,2,0:T(2,128)}, ...), condition=%wide.region_7.8_spmd, body=%wide.region_6.7_spmd.sunk | while | flops 15573277 | bytes 5088207 | solution.py:191
  515.6 10.6 fusion.347
  565.3 10.6 fusion.347
  639.4 125.4 %while.57 = (s32[]{:T(128)}, f32[4,4,2,2,32]{4,1,3,2,0:T(4,128)}, s32[4]{0:T(128)S(1)}, f32[10,10,512]{2,1,0:T(8,128)S(1)}, f32[4,316,4,2]{1,3,2,0:T(2,128)S(1)}...) while((s32[]{:T(128)}, f32[4,4,2,2,32]{4,1,3,2,0:T(4,128)}, ...), condition=%wide.region_5.6_spmd, body=%wide.region_4.5_spmd.sunk | while | flops 62293016 | bytes 10482019 | solution.py:191
  769.4 5.6 fusion.156
  776.5 4.5 collective-permute-start.2
  782.4 14.7 fusion.153
  797.1 10.9 copy.764
  808.1 8.3 reshape.355
  819.8 880.1 %while.56 = (s32[]{:T(128)}, f32[8,8,4,2,32]{4,1,3,2,0:T(8,128)}, s32[8]{0:T(128)S(1)}, f32[14,14,640]{2,1,0:T(8,128)S(1)}, f32[8,316,8,4]{1,3,2,0:T(4,128)}, /*...) while((s32[]{:T(128)}, f32[8,8,4,2,32]{4,1,3,2,0:T(8,128)}, ...), condition=%wide.region_3.4_spmd, body=%wide.region_2.3_spmd.sunk | while | flops 249172000 | bytes 36971048 | solution.py:191
  886.9 4.1 broadcast_multiply_fusion.41
  897.3 4.1 broadcast_multiply_fusion.42
  907.7 4.1 broadcast_multiply_fusion.43
  996.9 4.1 broadcast_multiply_fusion.41
  1007.3 4.1 broadcast_multiply_fusion.42
  1017.7 4.1 broadcast_multiply_fusion.43
  1106.9 4.1 broadcast_multiply_fusion.41
  1117.2 4.1 broadcast_multiply_fusion.42
  1127.6 4.1 broadcast_multiply_fusion.43
  1216.8 4.1 broadcast_multiply_fusion.41
  1227.2 4.1 broadcast_multiply_fusion.42
  1237.6 4.1 broadcast_multiply_fusion.43
  1326.8 4.1 broadcast_multiply_fusion.41
  1337.2 4.1 broadcast_multiply_fusion.42
  1347.5 4.1 broadcast_multiply_fusion.43
  1436.8 4.1 broadcast_multiply_fusion.41
  1447.1 4.1 broadcast_multiply_fusion.42
  1457.5 4.1 broadcast_multiply_fusion.43
  1546.7 4.1 broadcast_multiply_fusion.41
  1557.1 4.1 broadcast_multiply_fusion.42
  1567.5 4.1 broadcast_multiply_fusion.43
  1656.7 4.1 broadcast_multiply_fusion.41
  1667.0 4.1 broadcast_multiply_fusion.42
  1701.9 42.0 %while.59 = (s32[]{:T(128)}, f32[8,2,32,16]{2,3,1,0:T(8,128)S(1)}, f32[8,6,3,32,16]{3,4,2,1,0:T(8,128)}, f32[8,32,2,216]{3,0,2,1:T(8,128)S(1)}, s32[]{:T(128)}) while((s32[]{:T(128)}, f32[8,2,32,16]{2,3,1,0:T(8,128)S(1)}, f32[8,6,3,32,16]{3,4,2,1,0:T(8,128)}, f32[8,32,2,216]{3,0,2,1:T(8,128)S(1)}, s32[]{:T(128)}) %tuple.1098), condition=%wide.region_9.10_spmd, body=%wide.region_8.9_spmd.sunk | while | flops 2683906 | bytes 690249 | solution.py:289
  (2785 shorter events, 1202.8 us)
Async XLA Ops:
  0.0 413.1 %copy-start = (f32[216,32]{0,1:T(8,128)S(1)}, f32[216,32]{0,1:T(8,128)}, u32[]{:S(2)}) copy-start(f32[216,32]{0,1:T(8,128)} %param.31) | copy-start | bytes 82948
  0.0 6.6 copy-start.13
  6.6 9.2 copy-start.11
  14.2 13.6 copy-start.2
  57.1 9.2 copy-start.11
  64.7 13.6 copy-start.2
  107.6 9.2 copy-start.11
  115.2 13.6 copy-start.2
  158.1 9.2 copy-start.11
  165.7 13.6 copy-start.2
  208.6 9.2 copy-start.11
  216.2 13.6 copy-start.2
  259.1 9.2 copy-start.11
  266.8 13.6 copy-start.2
  309.7 9.2 copy-start.11
  317.3 13.6 copy-start.2
  360.2 9.2 copy-start.11
  367.8 13.6 copy-start.2
  411.0 9.5 copy-start.8
  415.5 359.5 %collective-permute-start = (f32[3,8,256]{2,1,0:T(8,128)}, f32[3,8,256]{2,1,0:T(8,128)}, u32[]{:S(2)}, u32[]{:S(2)}) collective-permute-start(f32[3,8,256]{2,1,0:T(8,128)} %slice.3106), channel_id=1, source_target_pairs={{0,4},{4,8},{8,12},{1,5},{5,9},{9,13},{2,6},{6,10},{10,14},{3,7},{... | collective-permute-start | bytes 73736 | tf_op jit(solution)/shard_map/ppermute | solution.py:25
  419.2 356.5 %collective-permute-start.1 = (f32[3,8,256]{2,1,0:T(8,128)}, f32[3,8,256]{2,1,0:T(8,128)}, u32[]{:S(2)}, u32[]{:S(2)}) collective-permute-start(f32[3,8,256]{2,1,0:T(8,128)} %slice.3108), channel_id=1, source_target_pairs={{4,0},{8,4},{12,8},{5,1},{9,5},{13,9},{6,2},{10,6},{14,10},{7,3},{... | collective-permute-start | bytes 73736 | tf_op jit(solution)/shard_map/ppermute | solution.py:27
  422.5 7.2 copy-start.24
  429.7 20.4 %copy-start.30 = (f32[2,6,6,1,1,1,1,1,1]{2,1,0,6,8,7,5,4,3:T(8,128)S(1)}, f32[2,6,6,1,1,1,1,1,1]{2,1,0,6,8,7,5,4,3:T(8,128)}, u32[]{:S(2)}) copy-start(f32[2,6,6,1,1,1,1,1,1]{2,1,0,6,8,7,5,4,3:T(8,128)} %constant.166) | copy-start | bytes 868
  450.2 6.5 copy-start.26
  461.7 157.8 %collective-permute-start.4 = (f32[3,4,128]{2,1,0:T(4,128)}, f32[3,4,128]{2,1,0:T(4,128)}, u32[]{:S(2)}, u32[]{:S(2)}) collective-permute-start(f32[3,4,128]{2,1,0:T(4,128)} %slice.3112), channel_id=1, source_target_pairs={{0,4},{4,8},{8,12},{1,5},{5,9},{9,13},{2,6},{6,10},{10,14},{3,7},{... | collective-permute-start | bytes 18440 | tf_op jit(solution)/shard_map/ppermute | solution.py:25
  467.5 152.7 %collective-permute-start.5 = (f32[3,4,128]{2,1,0:T(4,128)}, f32[3,4,128]{2,1,0:T(4,128)}, u32[]{:S(2)}, u32[]{:S(2)}) collective-permute-start(f32[3,4,128]{2,1,0:T(4,128)} %slice.3114), channel_id=1, source_target_pairs={{4,0},{8,4},{12,8},{5,1},{9,5},{13,9},{6,2},{10,6},{14,10},{7,3},{... | collective-permute-start | bytes 18440 | tf_op jit(solution)/shard_map/ppermute | solution.py:27
  473.7 36.6 %copy-start.31 = (s32[4,316]{1,0:T(4,128)S(1)}, s32[4,316]{1,0:T(4,128)}, u32[]{:S(2)}) copy-start(s32[4,316]{1,0:T(4,128)} %param.29) | copy-start | bytes 15172
  612.1 7.3 copy-start.15
  612.1 12.6 copy-start.21
  619.4 8.0 copy-start.10
  621.5 16.7 collective-permute-start.6
  623.4 14.9 collective-permute-start.7
  627.4 7.6 copy-start.23
  639.4 125.4 %copy-start.16 = (f32[216,32]{0,1:T(8,128)S(1)}, f32[216,32]{0,1:T(8,128)}, u32[]{:S(2)}) copy-start(f32[216,32]{0,1:T(8,128)} %param.32) | copy-start | bytes 82948
  639.4 10.2 copy-start.32
  670.7 10.2 copy-start.32
  702.0 10.2 copy-start.32
  733.3 10.2 copy-start.32
  769.4 13.0 copy-start.25
  776.5 39.8 %collective-permute-start.2 = (f32[14,3,256]{2,1,0:T(4,128)S(1)}, f32[14,3,256]{2,1,0:T(4,128)S(1)}, u32[]{:S(2)}, u32[]{:S(2)}) collective-permute-start(f32[14,3,256]{2,1,0:T(4,128)S(1)} %get-tuple-element.1309), channel_id=1, source_target_pairs={{0,1},{1,2},{2,3},{4,5},{5,6},{6,7},{8,9},{9,10},{10,11},{12,13},{... | collective-permute-start | bytes 129032 | tf_op jit(solution)/shard_map/ppermute | solution.py:25
  781.1 35.2 %collective-permute-start.3 = (f32[14,3,256]{2,1,0:T(4,128)S(1)}, f32[14,3,256]{2,1,0:T(4,128)S(1)}, u32[]{:S(2)}, u32[]{:S(2)}) collective-permute-start(f32[14,3,256]{2,1,0:T(4,128)S(1)} %get-tuple-element.1310), channel_id=1, source_target_pairs={{1,0},{2,1},{3,2},{5,4},{6,5},{7,6},{9,8},{10,9},{11,10},{13,12},{... | collective-permute-start | bytes 129032 | tf_op jit(solution)/shard_map/ppermute | solution.py:27
  869.8 16.1 copy-start.4
  877.1 5.4 copy-start.7
  877.1 9.7 copy-start.3
  979.7 16.1 copy-start.4
  987.1 5.4 copy-start.7
  987.1 9.7 copy-start.3
  1089.7 16.1 copy-start.4
  1097.1 5.4 copy-start.7
  1097.1 9.6 copy-start.3
  1199.7 16.1 copy-start.4
  1207.0 5.4 copy-start.7
  1207.0 9.6 copy-start.3
  1309.6 16.1 copy-start.4
  1317.0 5.4 copy-start.7
  1317.0 9.6 copy-start.3
  1419.6 16.1 copy-start.4
  1426.9 5.4 copy-start.7
  1426.9 9.7 copy-start.3
  1529.5 16.1 copy-start.4
  1536.9 5.4 copy-start.7
  1536.9 9.7 copy-start.3
  1639.5 16.1 copy-start.4
  1646.9 9.6 copy-start.3
  (42 other events, 121.9 us)
where the time goes:
time: 1770 us; the launch traced here: 1750 us
  local copies, waits for them, and re-layouts  984 us (56%)
  matrix products  496 us (28%)
  other arithmetic  179 us (10%)
  blocking collectives  34 us (2%)
  loops' own time  32.5 us (2%)
  starting transfers between devices  19.6 us (1%)
    while x1948, local copies, waits for them, and re-layouts  506 us
    another operation x106, local copies, waits for them, and re-layouts, one_plane(): jnp.stack(pieces).reshape(len(chosen), span_z, span_y, rhs_count, rank_size)  135 us
    mul x92, other arithmetic, one_plane(): stacked = stacked * mask_plane[first:last, :, :, None, None]  126 us
    dot_general x98, matrix products, one_plane(): jnp.einsum('ozyrk,oik->zyri', stacked, translations[first:last], precisio...  126 us
    dot_general x8, matrix products, multipole_block(): jnp.einsum('als,bls,cls,rls->lrabc', interp[:, 0], interp[:, 1], derivati...  101 us
    dot_general x8, matrix products, multipole_block(): jnp.einsum('als,bls,cls,rls->lrabc', derivative[:, 0], interp[:, 1], inte...  92.1 us
    dot_general x8, matrix products, multipole_block(): jnp.einsum('als,bls,cls,rls->lrabc', interp[:, 0], derivative[:, 1], inte...  83.7 us
    reshape x36, local copies, waits for them, and re-layouts, one_plane(): jnp.stack(pieces).reshape(len(chosen), span_z, span_y, rhs_count, rank_size)  79.6 us
  transfers between devices with their start and end apart: 8, of which 0 were waited for; matrix products, arithmetic and copies ran while one was open for 19% of the time, Pallas kernels for 0%

commit v1 on v0

v1 whole, which is shorter than its diff:
```python
import functools

import jax
import jax.numpy as jnp
import ml_dtypes
import numpy as np
from jax import lax
from jax.experimental import pallas as pl
from jax.experimental.pallas import tpu as pltpu
from jax.sharding import PartitionSpec as P

ORDER = 6
NODES = ORDER**3
RANK = 32
RHS = 2
BX, BZ, SY = 8, 8, 4
PCAP = 16
LEAVES = BX * BZ * SY
CHUNK = 256
f32 = jnp.float32
bf16 = jnp.bfloat16
VMEM_LIMIT = 56 * 1024 * 1024


def np_split(values):
    high = values.astype(np.float32).astype(ml_dtypes.bfloat16)
    low = (values - high.astype(np.float64)).astype(np.float32).astype(ml_dtypes.bfloat16)
    return high, low


def basis_table():
    angles = (2.0 * np.arange(ORDER) + 1.0) * np.pi / (2.0 * ORDER)
    degrees = np.arange(ORDER)
    weights = np.where(degrees == 0, 1.0, 2.0) / ORDER
    return np.cos(angles[:, None] * degrees[None, :]) * weights[None, :], np.cos(angles)


def basis_expander():
    table, _ = basis_table()
    full = np.zeros((3, NODES, ORDER, 8))
    for node in range(NODES):
        parts = (node // 36, node // 6 % 6, node % 6)
        for dim in range(3):
            full[dim, node, :, dim] = table[parts[dim]]
    high, low = np_split(full.reshape(3 * NODES, ORDER * 8))
    return np.concatenate([high, low, high], axis=1)


def child_kron():
    table, nodes = basis_table()
    sides = []
    for side in range(2):
        inside = (nodes + 2 * side - 1.0) / 2.0
        terms = np.cos(np.arange(ORDER)[:, None] * np.arccos(inside)[None, :])
        sides.append(table @ terms)
    stack = []
    for hx in range(2):
        for hz in range(2):
            for hy in range(2):
                full = np.einsum("ia,jb,lc->ijlabc", sides[hx], sides[hy], sides[hz])
                stack.append(full.reshape(NODES, NODES))
    return np.stack(stack)


def leaf_column(x, z, y, r):
    child = (x % 2) * 4 + (z % 2) * 2 + y % 2
    return child * 64 + parent_column(x // 2, z // 2, y // 2, r)


def parent_column(x, z, y, r):
    inner = (x % 2) * 4 + (z % 2) * 2 + y % 2
    return inner * 8 + r * 4 + (x // 2) * 2 + z // 2


@functools.lru_cache(None)
def tables():
    out = {}
    code = np.zeros((1, 512), np.int32)
    perm_leaf = np.zeros((512, 512), np.float32)
    perm_parent = np.zeros((64, 256), np.float32)
    perm_top = np.zeros((8, 128), np.float32)
    place = np.zeros((8, 192, 256), np.float32)
    target = np.full((2, 7, 7, 128), -1, np.int32)
    back = np.zeros((4, 128, 512), np.float32)
    back_parent = np.zeros((128, 64), np.float32)
    back_top = np.zeros((128, 8), np.float32)
    select = np.zeros((LEAVES, 512), np.float32)
    select_parent = np.zeros((32, 128), np.float32)
    select_top = np.zeros((4, 128), np.float32)
    for r in range(2):
        for x in range(8):
            for z in range(8):
                for y in range(4):
                    box = x * 32 + z * 4 + y
                    column = leaf_column(x, z, y, r)
                    code[0, column] = box * 2 + r
                    perm_leaf[column, x * 64 + r * 32 + z * 4 + y] = 1
                    half, inner = x // 4, x % 4
                    lane = half * 64 + r * 32 + z * 4 + y
                    back[inner, lane, column] = 1
                    select[box, inner * 128 + lane] = 1
                    for sy in range(7):
                        for sz in range(7):
                            yy, ze = y + sy - 3, z + sz - 1
                            if 0 <= yy < 4 and 0 <= ze < 12:
                                target[0, sy, sz, lane] = half * 128 + r * 48 + ze * 4 + yy
        for x in range(4):
            for z in range(4):
                for y in range(2):
                    column = parent_column(x, z, y, r)
                    perm_parent[column, x * 64 + r * 8 + z * 2 + y] = 1
                    lane = x * 16 + r * 8 + z * 2 + y
                    back_parent[lane, column] = 1
                    select_parent[x * 8 + z * 2 + y, lane] = 1
                    for sy in range(7):
                        for sz in range(7):
                            yy, ze = y + sy - 3, z + sz - 1
                            if 0 <= yy < 2 and 0 <= ze < 8:
                                target[1, sy, sz, lane] = x * 32 + r * 16 + ze * 2 + yy
        for x in range(2):
            for z in range(2):
                column = r * 4 + x * 2 + z
                perm_top[column, x * 64 + r * 2 + z] = 1
                lane = 64 + x * 4 + r * 2 + z
                back_top[lane, column] = 1
                select_top[x * 2 + z, lane] = 1
                for sz in range(7):
                    ze = z + sz - 1
                    if 0 <= ze < 6:
                        target[1, 3, sz, lane] = 128 + x * 16 + r * 6 + ze
        for half in range(2):
            for ze in range(12):
                for y in range(4):
                    slab, z = (ze + 6) // 8, (ze + 6) % 8
                    place[half, slab * 64 + r * 32 + z * 4 + y, half * 128 + r * 48 + ze * 4 + y] = 1
        for x in range(4):
            for ze in range(8):
                for y in range(2):
                    slab, z = (ze + 2) // 4, (ze + 2) % 4
                    place[2 + x, slab * 64 + r * 8 + z * 2 + y, x * 32 + r * 16 + ze * 2 + y] = 1
        for x in range(2):
            for ze in range(6):
                slab, z = ze // 2, ze % 2
                place[6 + x, slab * 64 + r * 2 + z, 128 + x * 16 + r * 6 + ze] = 1
    pad = np.zeros((343, 316), np.float32)
    index = 0
    for full in range(343):
        shifts = (full // 49 - 3, full // 7 % 7 - 3, full % 7 - 3)
        if max(abs(s) for s in shifts) > 1:
            pad[full, index] = 1
            index += 1
    low = lambda a: a.astype(ml_dtypes.bfloat16)
    kron = child_kron()
    out["kron"] = np.stack(np_split(kron))
    out["kron_t"] = np.stack(np_split(np.swapaxes(kron, 1, 2)))
    out["expander"] = basis_expander()
    out["code"] = code
    out["target"] = target
    for name, table in (
        ("perm_leaf", perm_leaf),
        ("perm_parent", perm_parent),
        ("perm_top", perm_top),
        ("place", place),
        ("back", back),
        ("back_parent", back_parent),
        ("back_top", back_top),
        ("select", select),
        ("select_parent", select_parent),
        ("select_top", select_top),
        ("pad", pad),
    ):
        out[name] = low(table)
    return out


def split(values):
    high = values.astype(bf16)
    return high, (values - high.astype(f32)).astype(bf16)


def dot(a, b):
    return jnp.dot(a, b, preferred_element_type=f32)


def dot2(a, exact):
    high, low = split(a)
    return dot(high, exact) + dot(low, exact)


def dot3(a, b):
    a_high, a_low = a
    b_high, b_low = b
    return dot(a_high, b_high) + dot(a_low, b_high) + dot(a_high, b_low)


def degree_rows(coords, normals):
    firsts = [jnp.ones_like(coords), coords]
    slopes = [jnp.zeros_like(coords), jnp.ones_like(coords)]
    for _ in range(2, ORDER):
        firsts.append(2.0 * coords * firsts[-1] - firsts[-2])
        slopes.append(2.0 * firsts[-2] + 2.0 * coords * slopes[-1] - slopes[-2])

    def rows(parts):
        high, low = split(jnp.concatenate(parts, axis=0))
        return jnp.concatenate([high, high, low], axis=0)

    if normals is None:
        return rows(firsts), None
    return rows(firsts), rows([slope * normals for slope in slopes])


def thirds(values):
    return values[:NODES], values[NODES : 2 * NODES], values[2 * NODES :]


def upward_kernel(
    coords, normals, charges, expander, code, kron, compress_t, perm_leaf, perm_parent, perm_top, out, poles
):
    poles[...] = jnp.zeros_like(poles)

    def chunk(step, _):
        lanes = pl.ds(pl.multiple_of(step * CHUNK, CHUNK), CHUNK)
        value_rows, slope_rows = degree_rows(coords[:, lanes], normals[:, lanes])
        sx, sy, sz = thirds(dot(expander[...], value_rows))
        dx, dy, dz = thirds(dot(expander[...], slope_rows))
        basis = dx * (sy * sz) + sx * (dy * sz + sy * dz)
        leaf = lax.broadcasted_iota(jnp.int32, (CHUNK, 512), 0) // PCAP + step * (CHUNK // PCAP)
        total = poles[...]
        for r in range(RHS):
            one_hot = (leaf * 2 + r == code[...]).astype(f32).astype(bf16)
            total = total + dot2(basis * charges[r : r + 1, lanes], one_hot)
        poles[...] = total
        return 0

    lax.fori_loop(0, coords.shape[1] // CHUNK, chunk, 0)
    weights = split(compress_t[...])
    leaf_poles = poles[...]
    leaf_coef = dot2(dot3(weights, split(leaf_poles)), perm_leaf[...])
    parent_poles = jnp.zeros((NODES, 64), f32)
    for h in range(8):
        parent_poles = parent_poles + dot3(
            (kron[0, h], kron[1, h]), split(leaf_poles[:, h * 64 : h * 64 + 64])
        )
    parent_coef = dot2(dot3(weights, split(parent_poles)), perm_parent[...])
    top_poles = jnp.zeros((NODES, 8), f32)
    for h in range(8):
        top_poles = top_poles + dot3(
            (kron[0, h], kron[1, h]), split(parent_poles[:, h * 8 : h * 8 + 8])
        )
    top_coef = dot2(dot3(weights, split(top_poles)), perm_top[...])
    for x in range(8):
        out[x] = leaf_coef[:, x * 64 : x * 64 + 64]
    for x in range(4):
        out[8 + x] = parent_coef[:, x * 64 : x * 64 + 64]
    for x in range(2):
        out[12 + x] = top_coef[:, x * 64 : x * 64 + 64]


def downward_kernel(
    full,
    place,
    target,
    operators,
    mask,
    back,
    back_parent,
    back_top,
    expand,
    kron_t,
    coords,
    expander,
    code_column,
    out,
    src_high,
    src_low,
    coarse_high,
    coarse_low,
    ops,
    parent_field,
    leaf_field,
    field_high,
    field_low,
):
    def load_ops(index, _):
        high, low = split(operators[index])
        ops[index, :32] = high
        ops[index, 32:] = low
        return 0

    lax.fori_loop(0, 49, load_ops, 0)

    def gathered(pieces, rows):
        high = jnp.zeros((rows, 256), f32)
        low = jnp.zeros((rows, 256), f32)
        for start, slot in pieces:
            part_high, part_low = split(full[start * 32 : start * 32 + rows])
            high = high + dot(part_high, place[slot])
            low = low + dot(part_low, place[slot])
        return high.astype(bf16), low.astype(bf16)

    leaf_src = gathered([(0, 0), (4, 1)], 256)
    coarse_src = gathered(
        [(12, 2), (13, 3), (14, 4), (15, 5), (22, 6), (23, 7)], 224
    )
    row_ids = lax.broadcasted_iota(jnp.int32, (256, 128), 0)
    for level, source, refs in (
        (0, leaf_src, (src_high, src_low)),
        (1, coarse_src, (coarse_high, coarse_low)),
    ):
        count = source[0].shape[0] // 32
        for sy in range(7):
            for sz in range(7):
                one_hot = (row_ids == target[level, sy, sz : sz + 1]).astype(f32).astype(bf16)
                for values, ref in zip(source, refs):
                    moved = dot(values, one_hot).astype(bf16)
                    ref[:, sy, sz * 32 : sz * 32 + 32] = moved.reshape(count, 32, 128)

    def shifted(high_ref, low_ref, xb, sx, first, carry):
        both, cross = carry
        for sy in range(7):
            rows = mask[sx, sy * 7 : sy * 7 + 7, first : first + 128]
            chosen = jnp.concatenate(
                [jnp.broadcast_to(rows[i : i + 1], (32, 128)) for i in range(7)], axis=0
            ).astype(bf16)
            weights = ops[sx * 7 + sy]
            both = both + dot(weights, high_ref[xb, sy] * chosen)
            cross = cross + dot(weights[:32], low_ref[xb, sy] * chosen)
        return both, cross

    def finish(carry):
        both, cross = carry
        return both[:32] + both[32:] + cross

    zeros = (jnp.zeros((64, 128), f32), jnp.zeros((32, 128), f32))
    leaf_local = jnp.zeros((32, 512), f32)
    for xi in range(4):
        begin = 1 - xi % 2

        def step(t, carry, xi=xi, begin=begin):
            sx = t + begin
            return shifted(src_high, src_low, xi + sx - 1, sx, xi * 128, carry)

        local = finish(lax.fori_loop(0, 6, step, zeros))
        leaf_local = leaf_local + dot2(local, back[xi])

    def coarse_step(sx, carry):
        return shifted(coarse_high, coarse_low, sx, sx, 512, carry)

    coarse = finish(lax.fori_loop(0, 7, coarse_step, zeros))
    weights = split(expand[...])
    top_field = dot3(weights, split(0.25 * dot2(coarse, back_top[...])))
    parent_own = dot3(weights, split(0.5 * dot2(coarse, back_parent[...])))
    parts = split(top_field)
    for h in range(8):
        cols = slice(h * 8, h * 8 + 8)
        parent_field[:, cols] = parent_own[:, cols] + dot3((kron_t[0, h], kron_t[1, h]), parts)
    leaf_own = dot3(weights, split(leaf_local))
    parts = split(parent_field[...])
    for h in range(8):
        cols = slice(h * 64, h * 64 + 64)
        leaf_field[:, cols] = leaf_own[:, cols] + dot3((kron_t[0, h], kron_t[1, h]), parts)
    field_high[...], field_low[...] = split(leaf_field[...])

    def chunk(index, _):
        lanes = pl.ds(pl.multiple_of(index * CHUNK, CHUNK), CHUNK)
        value_rows, _ = degree_rows(coords[:, lanes], None)
        sx, sy, sz = thirds(dot(expander[...], value_rows))
        basis = sx * (sy * sz)
        leaf = lax.broadcasted_iota(jnp.int32, (512, CHUNK), 1) // PCAP + index * (CHUNK // PCAP)
        for r in range(RHS):
            one_hot = (leaf * 2 + r == code_column[...]).astype(f32).astype(bf16)
            at_points = dot(field_high[...], one_hot) + dot(field_low[...], one_hot)
            out[r : r + 1, lanes] = jnp.sum(basis * at_points, axis=0, keepdims=True)
        return 0

    lax.fori_loop(0, coords.shape[1] // CHUNK, chunk, 0)


def neighbours(tail, head, axis):
    count = lax.axis_size(axis)
    before = lax.ppermute(tail, axis, [(i, i + 1) for i in range(count - 1)])
    after = lax.ppermute(head, axis, [(i + 1, i) for i in range(count - 1)])
    return before, after


def body(
    point_coords,
    point_normals,
    strengths,
    point_counts,
    leaf_list,
    parent_list,
    summit_list,
    translations,
    compress,
    expand,
):
    t = {name: jnp.asarray(value) for name, value in tables().items()}
    points = point_coords.shape[1]
    vmem = pl.BlockSpec(memory_space=pltpu.VMEM)
    params = pltpu.CompilerParams(vmem_limit_bytes=VMEM_LIMIT)
    coords = jnp.pad(point_coords, ((0, 5), (0, 0)))
    normals = jnp.pad(point_normals, ((0, 5), (0, 0)))
    slots = jnp.arange(PCAP, dtype=jnp.int32)[None, :] < point_counts.reshape(-1, 1)
    charges = jnp.where(slots.reshape(1, points), strengths, 0.0)

    coef = pl.pallas_call(
        upward_kernel,
        out_shape=jax.ShapeDtypeStruct((14, RANK, 64), f32),
        in_specs=[vmem] * 10,
        out_specs=vmem,
        scratch_shapes=[pltpu.VMEM((NODES, 512), f32)],
        compiler_params=params,
    )(
        coords,
        normals,
        charges,
        t["expander"],
        t["code"],
        t["kron"],
        compress.T,
        t["perm_leaf"],
        t["perm_parent"],
        t["perm_top"],
    )

    tail = jnp.concatenate([coef[6:8], coef[10:14]])
    head = jnp.concatenate([coef[0:2], coef[8:10], coef[12:14]])
    before, after = neighbours(tail, head, "block")
    blank = jnp.zeros_like(coef[:1])
    ext = jnp.concatenate(
        [before[0:2], coef[0:8], after[0:2], blank, before[2:4], coef[8:12], after[2:4], blank]
        + [blank, before[4:6], coef[12:14], after[4:6], blank]
    )
    left, right = neighbours(ext, ext, "slab")
    full = jnp.concatenate([left, ext, right], axis=2).reshape(30 * RANK, 192)

    def chosen(listing, select):
        return jnp.einsum("bo,bl->ol", listing.astype(bf16), select, preferred_element_type=f32)

    masks = jnp.concatenate(
        [
            chosen(leaf_list, t["select"]),
            chosen(parent_list, t["select_parent"]) + chosen(summit_list, t["select_top"]),
        ],
        axis=1,
    ).astype(bf16)
    masks = jnp.dot(t["pad"], masks, preferred_element_type=f32).reshape(7, 49, 640)
    pieces, index = [], 0
    near = [n for n in range(343) if not tables()["pad"][n].astype(np.float32).any()]
    position = 0
    while position < 343:
        stop = position
        if position in near:
            while stop in near:
                stop += 1
            pieces.append(jnp.zeros((stop - position, RANK, RANK), f32))
        else:
            while stop < 343 and stop not in near:
                stop += 1
            pieces.append(translations[index : index + stop - position])
            index += stop - position
        position = stop
    operators = jnp.concatenate(pieces).reshape(49, 7, RANK, RANK)
    operators = jnp.transpose(operators, (0, 2, 1, 3)).reshape(49, RANK, 7 * RANK)

    return pl.pallas_call(
        downward_kernel,
        out_shape=jax.ShapeDtypeStruct((RHS, points), f32),
        in_specs=[vmem] * 13,
        out_specs=vmem,
        scratch_shapes=[
            pltpu.VMEM((8, 7, 224, 128), bf16),
            pltpu.VMEM((8, 7, 224, 128), bf16),
            pltpu.VMEM((7, 7, 224, 128), bf16),
            pltpu.VMEM((7, 7, 224, 128), bf16),
            pltpu.VMEM((49, 64, 224), bf16),
            pltpu.VMEM((NODES, 64), f32),
            pltpu.VMEM((NODES, 512), f32),
            pltpu.VMEM((NODES, 512), bf16),
            pltpu.VMEM((NODES, 512), bf16),
        ],
        compiler_params=params,
    )(
        full,
        t["place"],
        t["target"],
        operators,
        masks,
        t["back"],
        t["back_parent"],
        t["back_top"],
        expand,
        t["kron_t"],
        coords,
        t["expander"],
        t["code"].reshape(512, 1),
    )


def solution(mesh):
    return jax.shard_map(
        body,
        mesh=mesh,
        in_specs=(
            P(None, ("groups", "block", "slab")),
            P(None, ("groups", "block", "slab")),
            P(None, ("groups", "block", "slab")),
            P(("groups", "block", "slab"), None),
            P(("groups", "block", "slab"), None),
            P(("groups", "block", "slab"), None),
            P(("groups", "block", "slab"), None),
            P(),
            P(),
            P(),
        ),
        out_specs=P(None, ("groups", "block", "slab")),
        check_vma=False,
    )
```

time: 1770 us -> 123 us (0.07); the launches traced: 1750 us -> 122 us
  local copies, waits for them, and re-layouts: 984 us -> 38.9 us
  matrix products: 496 us -> 1.89 us
  other arithmetic: 179 us -> 4.76 us
  Pallas kernels: 0 us -> 53.6 us
  blocking collectives: 34 us -> 0 us
  loops' own time: 32.5 us -> 0 us
    while x1951 -> x0, local copies, waits for them, and re-layouts: 512 us -> none
    dot_general x164 -> x4, matrix products: 496 us -> 1.89 us  [the longest x3 1.43 us: chosen(): jnp.einsum('bo,bl->ol', listing.astype(bf16), select, preferred_element_t...]
    another operation x109 -> x1, local copies, waits for them, and re-layouts: 142 us -> 0.05 us  [the longest x106 135 us: one_plane(): jnp.stack(pieces).reshape(len(chosen), span_z, span_y, rhs_count, rank_size)]
    mul x100 -> x0, other arithmetic: 132 us -> none  [the longest x92 126 us: one_plane(): stacked = stacked * mask_plane[first:last, :, :, None, None]]
    reshape x60 -> x2, local copies, waits for them, and re-layouts: 111 us -> 5.19 us  [the longest x1 4.09 us: body(): jnp.transpose(operators, (0, 2, 1, 3)).reshape(49, RANK, 7 * RANK)]
    mul x108 -> x0, local copies, waits for them, and re-layouts: 72.7 us -> none  [the longest x100 72.7 us: one_plane(): stacked = stacked * mask_plane[first:last, :, :, None, None]]
    pallas_call x0 -> x2, Pallas kernels: none -> 53.6 us  [the longest x1 35.8 us: body(): pl.pallas_call(downward_kernel, out_shape=jax.ShapeDtypeStruct((RHS, poin...]
    squeeze x88 -> x0, local copies, waits for them, and re-layouts: 42 us -> none  [the longest x16 17.8 us: multipole_block(): derivative[:, 2]]
  transfers between devices with their start and end apart: 8 -> 4, of which waited for: 0 -> 2; matrix products, arithmetic and copies ran while one was open for 19% -> 28% of each run, Pallas kernels for 0% -> 0%
where the time goes in v1:
time: 123 us; the launch traced here: 122 us
  Pallas kernels  53.6 us (44%)
  local copies, waits for them, and re-layouts  38.9 us (32%)
  starting transfers between devices  11.5 us (9%)
  waiting for transfers between devices  11.4 us (9%)
  other arithmetic  4.76 us (4%)
  matrix products  1.89 us (2%)
    pallas_call x1, Pallas kernels, body(): pl.pallas_call(downward_kernel, out_shape=jax.ShapeDtypeStruct((RHS, poin...  35.8 us
    pallas_call x1, Pallas kernels, body(): pl.pallas_call(upward_kernel, out_shape=jax.ShapeDtypeStruct((14, RANK, 6...  17.8 us
    concatenate x2, local copies, waits for them, and re-layouts, body(): operators = jnp.concatenate(pieces).reshape(49, 7, RANK, RANK)  12.8 us
    ppermute x2, starting transfers between devices, neighbours(): before = lax.ppermute(tail, axis, [(i, i + 1) for i in range(count - 1)])  8.74 us
    ppermute x2, waiting for transfers between devices, neighbours(): before = lax.ppermute(tail, axis, [(i, i + 1) for i in range(count - 1)])  7.28 us
    transpose x1, local copies, waits for them, and re-layouts, body(): jnp.transpose(operators, (0, 2, 1, 3)).reshape(49, RANK, 7 * RANK)  6 us
    unnamed x34, local copies, waits for them, and re-layouts  5.38 us
    slice x3, local copies, waits for them, and re-layouts, body(): pieces.append(translations[index:index + stop - position])  4.66 us
  transfers between devices with their start and end apart: 4, of which 2 were waited for; matrix products, arithmetic and copies ran while one was open for 28% of the time, Pallas kernels for 0%

profile of v1, /device:TPU:0, one launch (start us, length us, event | category | flops | bytes accessed | tf_op | source)
XLA Modules:
  0.0 122.2 jit_solution(15090620023107778040)
XLA Ops:
  0.0 1.5 %pad.7.coords = f32[8,4096]{1,0:T(8,128)} pad(f32[3,4096]{1,0:T(4,128)} %param.26, f32[]{:T(128)} %constant.17.clone.1), padding=0_5x0_0 | pad | bytes 180228 | tf_op jit(solution)/shard_map/jit(_pad)/pad | solution.py:402
  1.5 1.5 %pad.8.normals = f32[8,4096]{1,0:T(8,128)} pad(f32[3,4096]{1,0:T(4,128)} %param.27, f32[]{:T(128)} %constant.17.clone.1), padding=0_5x0_0 | pad | bytes 180228 | tf_op jit(solution)/shard_map/jit(_pad)/pad | solution.py:403
  3.0 0.8 iota_compare_fusion
  3.8 0.1 lt.26
  3.9 1.4 %broadcast_select_fusion.charges = f32[2,4096]{1,0:T(2,128)} fusion(f32[2,4096]{1,0:T(2,128)} %param.28, pred[4096]{0:T(1024)(128)(4,1)S(1)} %lt.26), kind=kLoop, calls=%fused_computation.22 | loop fusion | flops 8192 | bytes 69632 | tf_op jit(solution)/shard_map/jit(_where)/select_n | solution.py:405
  5.3 0.0 copy-start
  5.3 17.8 %shard_map.244 = f32[14,32,64]{2,1,0:T(8,128)} custom-call(f32[8,4096]{1,0:T(8,128)} %pad.7.coords, f32[8,4096]{1,0:T(8,128)} %pad.8.normals, f32[2,4096]{1,0:T(2,128)} %broadcast_select_fusion.charges, bf16[648,144]{1,0:T(8,128)(2,1)} %constant.20.clone.expander, s32[1,512]{1,0:T(1,128)} %constant.42.clone.code, ...), custom_call_target="tpu_custom_call" | custom-call | tf_op jit(solution)/shard_map/pallas_call | solution.py:407
  23.1 0.8 fusion.15
  23.9 0.6 pad_maximum_fusion.2
  24.6 1.3 %collective-permute-start.1 = (f32[6,32,64]{2,1,0:T(8,128)}, f32[6,32,64]{2,1,0:T(8,128)}, u32[]{:S(2)}, u32[]{:S(2)}) collective-permute-start(f32[6,32,64]{2,1,0:T(8,128)} %pad_maximum_fusion.2), channel_id=1, source_target_pairs={{4,0},{8,4},{12,8},{5,1},{9,5},{13,9},{6,2},{10,6},{14,10},{7,3},{... | collective-permute-start | bytes 147464 | tf_op jit(solution)/shard_map/ppermute | solution.py:382
  25.8 0.8 slice.94
  26.7 0.7 pad_maximum_fusion.1
  27.3 3.7 %collective-permute-start = (f32[6,32,64]{2,1,0:T(8,128)}, f32[6,32,64]{2,1,0:T(8,128)}, u32[]{:S(2)}, u32[]{:S(2)}) collective-permute-start(f32[6,32,64]{2,1,0:T(8,128)} %pad_maximum_fusion.1), channel_id=1, source_target_pairs={{0,4},{4,8},{8,12},{1,5},{5,9},{9,13},{2,6},{6,10},{10,14},{3,7},{... | collective-permute-start | bytes 147464 | tf_op jit(solution)/shard_map/ppermute | solution.py:381
  31.0 0.0 copy-done
  31.0 2.2 %fusion.13 = (f32[4,32,32]{0,2,1:T(8,128)S(1)}, f32[4,32,32]{0,2,1:T(8,128)S(1)}, f32[4,32,32]{0,2,1:T(8,128)}, f32[4,32,32]{0,2,1:T(8,128)}, f32[4,32,32]{0,2,1:T(8,128)}, /*index=5*/f32[4,32,32]{0,2,1:T(8,128)}) fusion(f32[316,32,32]{0,2,1:T(8,128)S(1)} %copy-done), kind=kLoop, calls=%fused_computation.32 | loop fusion | bytes 196608 | tf_op jit(solution)/shard_map/slice | solution.py:461
  33.2 0.0 copy-start.3
  33.2 0.0 copy-start.5
  33.2 1.3 %fusion.14 = (f32[32,32,32]{0,2,1:T(8,128)}, f32[32,32,32]{0,2,1:T(8,128)}) fusion(f32[316,32,32]{0,2,1:T(8,128)S(1)} %copy-done), kind=kLoop, calls=%fused_computation.33 | loop fusion | bytes 524288 | tf_op jit(solution)/shard_map/slice | solution.py:461
  34.5 0.0 copy-start.6
  34.5 0.0 copy-start.8
  34.5 0.0 copy-start.9
  34.5 0.0 copy-start.10
  34.5 1.1 fusion.12
  35.7 0.0 copy-done.3
  35.7 0.0 copy-done.5
  35.7 0.3 fusion
  36.0 0.0 copy-done.6
  36.0 0.0 copy-done.8
  36.1 0.2 fusion.8
  36.3 0.0 copy-done.9
  36.3 0.0 copy-done.10
  36.3 0.9 fusion.2
  37.2 7.1 %concatenate.27 = f32[343,32,32]{0,2,1:T(8,128)S(1)} concatenate(f32[114,32,32]{0,2,1:T(8,128)} %get-tuple-element.6, f32[3,32,32]{0,2,1:T(8,128)S(1)} %broadcast.11, f32[4,32,32]{0,2,1:T(8,128)} %get-tuple-element.12, f32[3,32,32]{0,2,1:T(8,128)S(1)} %broadcast.11, f32[4,32,32]{0,2,1:T(8,128)} %get-tuple-element.11, f32[3,32,32]{0,2,1:T(8,128)S(1)} %broadcast.11, ...), dimensions={0} | concatenate | bytes 2809856 | tf_op jit(solution)/shard_map/concatenate | solution.py:464
  44.3 5.8 %copy.29 = f32[343,32,32]{2,1,0:T(8,128)} copy(f32[343,32,32]{0,2,1:T(8,128)S(1)} %concatenate.27) | data formatting | bytes 2809856 | tf_op jit(solution)/shard_map/concatenate | solution.py:464
  50.1 6.0 %copy.30 = f32[49,32,7,32]{0,3,2,1:T(8,128)} copy(f32[49,32,7,32]{3,1,2,0:T(8,128)} %bitcast.15) | data formatting | bytes 2809856 | tf_op jit(solution)/shard_map/transpose | solution.py:465
  56.1 0.0 copy-start.1
  56.1 0.0 copy-start.2
  56.1 0.0 copy-start.4
  56.1 4.1 %copy.31.operators = f32[49,32,224]{2,1,0:T(8,128)} copy(f32[49,32,224]{0,2,1:T(8,128)} %bitcast.16) | data formatting | bytes 2809856 | tf_op jit(solution)/shard_map/reshape | solution.py:465
  60.2 0.0 collective-permute-done
  60.2 0.8 slice_dynamic-update-slice_fusion.7
  60.9 0.0 copy-done.1
  60.9 0.0 collective-permute-done.1
  60.9 0.8 slice_dynamic-update-slice_fusion.6
  61.7 0.8 slice_dynamic-update-slice_fusion.5
  62.5 0.8 slice_dynamic-update-slice_fusion.4
  63.3 0.8 slice_dynamic-update-slice_fusion.3
  64.0 0.8 slice_dynamic-update-slice_fusion.2
  64.8 0.0 copy-start.7
  64.8 5.1 %collective-permute-start.2 = (f32[30,32,64]{2,1,0:T(8,128)S(1)}, f32[30,32,64]{2,1,0:T(8,128)S(1)}, u32[]{:S(2)}, u32[]{:S(2)}) collective-permute-start(f32[30,32,64]{2,1,0:T(8,128)S(1)} %constant_dynamic-update-slice_fusion), channel_id=1, source_target_pairs={{0,1},{1,2},{2,3},{4,5},{5,6},{6,7},{8,9},{9,10},{10,11},{12,13},{... | collective-permute-start | bytes 737288 | tf_op jit(solution)/shard_map/ppermute | solution.py:381
  69.9 1.5 %collective-permute-start.3 = (f32[30,32,64]{2,1,0:T(8,128)S(1)}, f32[30,32,64]{2,1,0:T(8,128)S(1)}, u32[]{:S(2)}, u32[]{:S(2)}) collective-permute-start(f32[30,32,64]{2,1,0:T(8,128)S(1)} %constant_dynamic-update-slice_fusion), channel_id=1, source_target_pairs={{1,0},{2,1},{3,2},{5,4},{6,5},{7,6},{9,8},{10,9},{11,10},{13,12},{... | collective-permute-start | bytes 737288 | tf_op jit(solution)/shard_map/ppermute | solution.py:382
  71.4 0.0 copy-done.2
  71.4 0.0 copy-done.4
  71.4 0.5 fusion.3
  71.8 1.1 reshape.35.mask
  72.9 0.0 copy-done.7
  72.9 0.7 copy.32.expand
  73.7 7.3 %collective-permute-done.2 = f32[30,32,64]{2,1,0:T(8,128)S(1)} collective-permute-done((f32[30,32,64]{2,1,0:T(8,128)S(1)}, f32[30,32,64]{2,1,0:T(8,128)S(1)}, u32[]{:S(2)}, u32[]{:S(2)}) %collective-permute-start.2) | collective-permute-done | bytes 245792 | tf_op jit(solution)/shard_map/ppermute | solution.py:381
  81.0 4.1 %collective-permute-done.3 = f32[30,32,64]{2,1,0:T(8,128)S(1)} collective-permute-done((f32[30,32,64]{2,1,0:T(8,128)S(1)}, f32[30,32,64]{2,1,0:T(8,128)S(1)}, u32[]{:S(2)}, u32[]{:S(2)}) %collective-permute-start.3) | collective-permute-done | bytes 245792 | tf_op jit(solution)/shard_map/ppermute | solution.py:382
  85.1 1.3 %pad_maximum_fusion = f32[30,32,192]{2,1,0:T(8,128)} fusion(f32[30,32,64]{2,1,0:T(8,128)S(1)} %collective-permute-done.3, f32[30,32,64]{2,1,0:T(8,128)S(1)} %constant_dynamic-update-slice_fusion, f32[30,32,64]{2,1,0:T(8,128)S(1)} %collective-permute-done.2), kind=kLoop, calls=%fused_computation.5 | loop fusion | flops 368640 | bytes 1474560 | tf_op jit(solution)/shard_map/concatenate | solution.py:436
  86.4 35.8 %shard_map.245 = f32[2,4096]{1,0:T(2,128)} custom-call(f32[960,192]{1,0:T(8,128)} %bitcast.17, bf16[8,192,256]{2,1,0:T(8,128)(2,1)} %constant.47.clone.place, s32[2,7,7,128]{3,2,1,0:T(8,128)} %constant.43.clone.target, f32[49,32,224]{2,1,0:T(8,128)} %copy.31.operators, f32[7,49,640]{2,1,0:T(8,128)} %reshape.35.mask, ...), custom_call_target="tpu_custom_call" | custom-call | tf_op jit(solution)/shard_map/pallas_call | solution.py:467
  (7 shorter events, 0.1 us)
Async XLA Ops:
  5.3 25.7 %copy-start = (f32[316,32,32]{0,2,1:T(8,128)S(1)}, f32[316,32,32]{0,2,1:T(8,128)}, u32[]{:S(2)}) copy-start(f32[316,32,32]{0,2,1:T(8,128)} %param.33) | copy-start | bytes 3883012
  24.6 36.4 %collective-permute-start.1 = (f32[6,32,64]{2,1,0:T(8,128)}, f32[6,32,64]{2,1,0:T(8,128)}, u32[]{:S(2)}, u32[]{:S(2)}) collective-permute-start(f32[6,32,64]{2,1,0:T(8,128)} %pad_maximum_fusion.2), channel_id=1, source_target_pairs={{4,0},{8,4},{12,8},{5,1},{9,5},{13,9},{6,2},{10,6},{14,10},{7,3},{... | collective-permute-start | bytes 147464 | tf_op jit(solution)/shard_map/ppermute | solution.py:382
  27.3 32.8 %collective-permute-start = (f32[6,32,64]{2,1,0:T(8,128)}, f32[6,32,64]{2,1,0:T(8,128)}, u32[]{:S(2)}, u32[]{:S(2)}) collective-permute-start(f32[6,32,64]{2,1,0:T(8,128)} %pad_maximum_fusion.1), channel_id=1, source_target_pairs={{0,4},{4,8},{8,12},{1,5},{5,9},{9,13},{2,6},{6,10},{10,14},{3,7},{... | collective-permute-start | bytes 147464 | tf_op jit(solution)/shard_map/ppermute | solution.py:381
  33.2 2.5 %copy-start.3 = (s32[256,316]{0,1:T(8,128)S(1)}, s32[256,316]{0,1:T(8,128)}, u32[]{:S(2)}) copy-start(s32[256,316]{0,1:T(8,128)} %param.30) | copy-start | bytes 970756
  33.2 2.5 %copy-start.5 = (bf16[256,512]{1,0:T(8,128)(2,1)S(1)}, bf16[256,512]{1,0:T(8,128)(2,1)}, u32[]{:S(2)}) copy-start(bf16[256,512]{1,0:T(8,128)(2,1)} %constant.51.clone) | copy-start | bytes 786436
  34.5 1.5 %copy-start.6 = (s32[32,316]{1,0:T(8,128)S(1)}, s32[32,316]{1,0:T(8,128)}, u32[]{:S(2)}) copy-start(s32[32,316]{1,0:T(8,128)} %param.31) | copy-start | bytes 121348
  34.5 1.5 %copy-start.8 = (bf16[32,128]{1,0:T(8,128)(2,1)S(1)}, bf16[32,128]{1,0:T(8,128)(2,1)}, u32[]{:S(2)}) copy-start(bf16[32,128]{1,0:T(8,128)(2,1)} %constant.52.clone) | copy-start | bytes 24580
  34.5 1.7 %copy-start.9 = (s32[4,316]{1,0:T(4,128)S(1)}, s32[4,316]{1,0:T(4,128)}, u32[]{:S(2)}) copy-start(s32[4,316]{1,0:T(4,128)} %param.32) | copy-start | bytes 15172
  34.5 1.7 %copy-start.10 = (bf16[4,128]{1,0:T(4,128)(2,1)S(1)}, bf16[4,128]{1,0:T(4,128)(2,1)}, u32[]{:S(2)}) copy-start(bf16[4,128]{1,0:T(4,128)(2,1)} %constant.53.clone) | copy-start | bytes 3076
  56.1 4.9 %copy-start.1 = (f32[14,32,64]{2,1,0:T(8,128)S(1)}, f32[14,32,64]{2,1,0:T(8,128)}, u32[]{:S(2)}) copy-start(f32[14,32,64]{2,1,0:T(8,128)} %shard_map.244) | copy-start | bytes 344068
  56.1 15.3 %copy-start.2 = (bf16[316,128]{0,1:T(8,128)(2,1)S(1)}, bf16[316,128]{0,1:T(8,128)(2,1)}, u32[]{:S(2)}) copy-start(bf16[316,128]{0,1:T(8,128)(2,1)} %fusion.2) | copy-start | bytes 242692
  56.1 15.3 %copy-start.4 = (bf16[343,316]{1,0:T(8,128)(2,1)S(1)}, bf16[343,316]{1,0:T(8,128)(2,1)}, u32[]{:S(2)}) copy-start(bf16[343,316]{1,0:T(8,128)(2,1)} %constant.54.clone) | copy-start | bytes 650332
  64.8 8.2 %copy-start.7 = (f32[216,32]{0,1:T(8,128)S(1)}, f32[216,32]{0,1:T(8,128)}, u32[]{:S(2)}) copy-start(f32[216,32]{0,1:T(8,128)} %param.35) | copy-start | bytes 82948
  64.8 16.2 %collective-permute-start.2 = (f32[30,32,64]{2,1,0:T(8,128)S(1)}, f32[30,32,64]{2,1,0:T(8,128)S(1)}, u32[]{:S(2)}, u32[]{:S(2)}) collective-permute-start(f32[30,32,64]{2,1,0:T(8,128)S(1)} %constant_dynamic-update-slice_fusion), channel_id=1, source_target_pairs={{0,1},{1,2},{2,3},{4,5},{5,6},{6,7},{8,9},{9,10},{10,11},{12,13},{... | collective-permute-start | bytes 737288 | tf_op jit(solution)/shard_map/ppermute | solution.py:381
  69.9 15.2 %collective-permute-start.3 = (f32[30,32,64]{2,1,0:T(8,128)S(1)}, f32[30,32,64]{2,1,0:T(8,128)S(1)}, u32[]{:S(2)}, u32[]{:S(2)}) collective-permute-start(f32[30,32,64]{2,1,0:T(8,128)S(1)} %constant_dynamic-update-slice_fusion), channel_id=1, source_target_pairs={{1,0},{2,1},{3,2},{5,4},{6,5},{7,6},{9,8},{10,9},{11,10},{13,12},{... | collective-permute-start | bytes 737288 | tf_op jit(solution)/shard_map/ppermute | solution.py:382

commit v2 on v1

--- a/solution.py
+++ b/solution.py
@@ -209,6 +209,10 @@
     return rows(firsts), rows([slope * normals for slope in slopes])
 
 
+def padded(values):
+    return jnp.concatenate([values, jnp.zeros((5, values.shape[1]), f32)], axis=0)
+
+
 def thirds(values):
     return values[:NODES], values[NODES : 2 * NODES], values[2 * NODES :]
 
@@ -220,7 +224,7 @@
 
     def chunk(step, _):
         lanes = pl.ds(pl.multiple_of(step * CHUNK, CHUNK), CHUNK)
-        value_rows, slope_rows = degree_rows(coords[:, lanes], normals[:, lanes])
+        value_rows, slope_rows = degree_rows(padded(coords[:, lanes]), padded(normals[:, lanes]))
         sx, sy, sz = thirds(dot(expander[...], value_rows))
         dx, dy, dz = thirds(dot(expander[...], slope_rows))
         basis = dx * (sy * sz) + sx * (dy * sz + sy * dz)
@@ -248,19 +252,153 @@
             (kron[0, h], kron[1, h]), split(parent_poles[:, h * 8 : h * 8 + 8])
         )
     top_coef = dot2(dot3(weights, split(top_poles)), perm_top[...])
-    for x in range(8):
-        out[x] = leaf_coef[:, x * 64 : x * 64 + 64]
-    for x in range(4):
-        out[8 + x] = parent_coef[:, x * 64 : x * 64 + 64]
-    for x in range(2):
-        out[12 + x] = top_coef[:, x * 64 : x * 64 + 64]
+    own = [leaf_coef[:, x * 64 : x * 64 + 64] for x in range(8)]
+    own += [parent_coef[:, x * 64 : x * 64 + 64] for x in range(4)]
+    own += [top_coef[:, x * 64 : x * 64 + 64] for x in range(2)]
+    own = [jnp.concatenate([part[:16], part[16:]], axis=1) for part in own]
+    order = [0, 1, 8, 9, 12, 13] + list(range(14)) + [6, 7, 10, 11, 12, 13]
+    for row, index in enumerate(order):
+        out[row] = own[index]
+
+
+def exchange_kernel(coef, out, land, send, recv):
+    block, slab = lax.axis_index("block"), lax.axis_index("slab")
+    blocks, slabs = lax.axis_size("block"), lax.axis_size("slab")
+    sides = (
+        (block > 0, {"block": block - 1}),
+        (block < blocks - 1, {"block": block + 1}),
+        (slab > 0, {"slab": slab - 1}),
+        (slab < slabs - 1, {"slab": slab + 1}),
+    )
+    mesh_ids = pl.DeviceIdType.MESH
+    barrier = pltpu.get_barrier_semaphore()
+    for there, device in sides:
+
+        @pl.when(there)
+        def _(device=device):
+            pl.semaphore_signal(barrier, inc=1, device_id=device, device_id_type=mesh_ids)
+
+    peers = sum(there.astype(jnp.int32) for there, _ in sides)
+    pl.semaphore_wait(barrier, peers)
+
+    def copy(src, dst, index, device):
+        return pltpu.make_async_remote_copy(
+            src_ref=src,
+            dst_ref=dst,
+            send_sem=send.at[index],
+            recv_sem=recv.at[index],
+            device_id=device,
+            device_id_type=mesh_ids,
+        )
+
+    to_left = copy(coef.at[0:6], land.at[1, 20:26], 0, sides[0][1])
+    to_right = copy(coef.at[20:26], land.at[1, 0:6], 1, sides[1][1])
+    own_down = copy(coef.at[6:20], land.at[2, 6:20], 2, sides[2][1])
+    own_up = copy(coef.at[6:20], land.at[0, 6:20], 3, sides[3][1])
+    low_down = copy(land.at[1, 0:6], land.at[2, 0:6], 4, sides[2][1])
+    low_up = copy(land.at[1, 0:6], land.at[0, 0:6], 5, sides[3][1])
+    high_down = copy(land.at[1, 20:26], land.at[2, 20:26], 6, sides[2][1])
+    high_up = copy(land.at[1, 20:26], land.at[0, 20:26], 7, sides[3][1])
+
+    @pl.when(sides[0][0])
+    def _():
+        to_left.start()
+
+    @pl.when(sides[1][0])
+    def _():
+        to_right.start()
+
+    @pl.when(sides[2][0])
+    def _():
+        own_down.start()
+
+    @pl.when(sides[3][0])
+    def _():
+        own_up.start()
+
+    land[1, 6:20] = coef[6:20]
+
+    @pl.when(block == 0)
+    def _():
+        land[1, 0:6] = jnp.zeros((6, 16, 128), f32)
+
+    @pl.when(block == blocks - 1)
+    def _():
+        land[1, 20:26] = jnp.zeros((6, 16, 128), f32)
+
+    @pl.when(slab == 0)
+    def _():
+        land[0] = jnp.zeros((26, 16, 128), f32)
+
+    @pl.when(slab == slabs - 1)
+    def _():
+        land[2] = jnp.zeros((26, 16, 128), f32)
+
+    @pl.when(sides[0][0])
+    def _():
+        to_right.wait_recv()
+
+    @pl.when(sides[1][0])
+    def _():
+        to_left.wait_recv()
+
+    @pl.when(sides[2][0])
+    def _():
+        low_down.start()
+        high_down.start()
+
+    @pl.when(sides[3][0])
+    def _():
+        low_up.start()
+        high_up.start()
+
+    @pl.when(sides[2][0])
+    def _():
+        own_up.wait_recv()
+        low_up.wait_recv()
+        high_up.wait_recv()
+
+    @pl.when(sides[3][0])
+    def _():
+        own_down.wait_recv()
+        low_down.wait_recv()
+        high_down.wait_recv()
+
+    out[...] = land[...]
+
+    @pl.when(sides[0][0])
+    def _():
+        to_left.wait_send()
+
+    @pl.when(sides[1][0])
+    def _():
+        to_right.wait_send()
+
+    @pl.when(sides[2][0])
+    def _():
+        own_down.wait_send()
+        low_down.wait_send()
+        high_down.wait_send()
+
+    @pl.when(sides[3][0])
+    def _():
+        own_up.wait_send()
+        low_up.wait_send()
+        high_up.wait_send()
+
+
+def source_rows():
+    leaf = [e if e < 2 else e + 4 if e < 10 else e + 10 for e in range(12)]
+    parent = [2 + e if e < 2 else 12 + e if e < 6 else 16 + e for e in range(8)]
+    top = [4 + e if e < 2 else 16 + e if e < 4 else 20 + e for e in range(6)]
+    return leaf + [None] + parent + [None, None] + top + [None]
 
 
 def downward_kernel(
-    full,
+    exchanged,
     place,
     target,
-    operators,
+    translations,
     mask,
     back,
     back_parent,
@@ -271,6 +409,8 @@
     expander,
     code_column,
     out,
+    full_high,
+    full_low,
     src_high,
     src_low,
     coarse_high,
@@ -281,21 +421,38 @@
     field_high,
     field_low,
 ):
-    def load_ops(index, _):
-        high, low = split(operators[index])
-        ops[index, :32] = high
-        ops[index, 32:] = low
-        return 0
-
-    lax.fori_loop(0, 49, load_ops, 0)
+    listed = 0
+    for pair in range(49):
+        pieces = []
+        for sz in range(7):
+            shifts = (pair // 7 - 3, pair % 7 - 3, sz - 3)
+            if max(abs(s) for s in shifts) > 1:
+                pieces.append(translations[listed])
+                listed += 1
+            else:
+                pieces.append(jnp.zeros((32, 32), f32))
+        high, low = split(jnp.concatenate(pieces, axis=1))
+        ops[pair, :32] = high
+        ops[pair, 32:] = low
+
+    for row, source in enumerate(source_rows()):
+        for half in range(2):
+            rows = slice(row * 32 + half * 16, row * 32 + half * 16 + 16)
+            if source is None:
+                full_high[rows] = jnp.zeros((16, 192), bf16)
+                full_low[rows] = jnp.zeros((16, 192), bf16)
+            else:
+                lanes = slice(half * 64, half * 64 + 64)
+                parts = [exchanged[slab, source, :, lanes] for slab in range(3)]
+                full_high[rows], full_low[rows] = split(jnp.concatenate(parts, axis=1))
 
     def gathered(pieces, rows):
         high = jnp.zeros((rows, 256), f32)
         low = jnp.zeros((rows, 256), f32)
         for start, slot in pieces:
-            part_high, part_low = split(full[start * 32 : start * 32 + rows])
-            high = high + dot(part_high, place[slot])
-            low = low + dot(part_low, place[slot])
+            part = slice(start * 32, start * 32 + rows)
+            high = high + dot(full_high[part], place[slot])
+            low = low + dot(full_low[part], place[slot])
         return high.astype(bf16), low.astype(bf16)
 
     leaf_src = gathered([(0, 0), (4, 1)], 256)
@@ -363,7 +520,7 @@
 
     def chunk(index, _):
         lanes = pl.ds(pl.multiple_of(index * CHUNK, CHUNK), CHUNK)
-        value_rows, _ = degree_rows(coords[:, lanes], None)
+        value_rows, _ = degree_rows(padded(coords[:, lanes]), None)
         sx, sy, sz = thirds(dot(expander[...], value_rows))
         basis = sx * (sy * sz)
         leaf = lax.broadcasted_iota(jnp.int32, (512, CHUNK), 1) // PCAP + index * (CHUNK // PCAP)
@@ -374,13 +531,6 @@
         return 0
 
     lax.fori_loop(0, coords.shape[1] // CHUNK, chunk, 0)
-
-
-def neighbours(tail, head, axis):
-    count = lax.axis_size(axis)
-    before = lax.ppermute(tail, axis, [(i, i + 1) for i in range(count - 1)])
-    after = lax.ppermute(head, axis, [(i + 1, i) for i in range(count - 1)])
-    return before, after
 
 
 def body(
@@ -399,21 +549,19 @@
     points = point_coords.shape[1]
     vmem = pl.BlockSpec(memory_space=pltpu.VMEM)
     params = pltpu.CompilerParams(vmem_limit_bytes=VMEM_LIMIT)
-    coords = jnp.pad(point_coords, ((0, 5), (0, 0)))
-    normals = jnp.pad(point_normals, ((0, 5), (0, 0)))
     slots = jnp.arange(PCAP, dtype=jnp.int32)[None, :] < point_counts.reshape(-1, 1)
     charges = jnp.where(slots.reshape(1, points), strengths, 0.0)
 
     coef = pl.pallas_call(
         upward_kernel,
-        out_shape=jax.ShapeDtypeStruct((14, RANK, 64), f32),
+        out_shape=jax.ShapeDtypeStruct((26, 16, 128), f32),
         in_specs=[vmem] * 10,
         out_specs=vmem,
         scratch_shapes=[pltpu.VMEM((NODES, 512), f32)],
         compiler_params=params,
     )(
-        coords,
-        normals,
+        point_coords,
+        point_normals,
         charges,
         t["expander"],
         t["code"],
@@ -424,16 +572,18 @@
         t["perm_top"],
     )
 
-    tail = jnp.concatenate([coef[6:8], coef[10:14]])
-    head = jnp.concatenate([coef[0:2], coef[8:10], coef[12:14]])
-    before, after = neighbours(tail, head, "block")
-    blank = jnp.zeros_like(coef[:1])
-    ext = jnp.concatenate(
-        [before[0:2], coef[0:8], after[0:2], blank, before[2:4], coef[8:12], after[2:4], blank]
-        + [blank, before[4:6], coef[12:14], after[4:6], blank]
-    )
-    left, right = neighbours(ext, ext, "slab")
-    full = jnp.concatenate([left, ext, right], axis=2).reshape(30 * RANK, 192)
+    exchanged = pl.pallas_call(
+        exchange_kernel,
+        out_shape=jax.ShapeDtypeStruct((3, 26, 16, 128), f32),
+        in_specs=[vmem],
+        out_specs=vmem,
+        scratch_shapes=[
+            pltpu.VMEM((3, 26, 16, 128), f32),
+            pltpu.SemaphoreType.DMA((8,)),
+            pltpu.SemaphoreType.DMA((8,)),
+        ],
+        compiler_params=pltpu.CompilerParams(collective_id=0, has_side_effects=True),
+    )(coef)
 
     def chosen(listing, select):
         return jnp.einsum("bo,bl->ol", listing.astype(bf16), select, preferred_element_type=f32)
@@ -446,30 +596,14 @@
         axis=1,
     ).astype(bf16)
     masks = jnp.dot(t["pad"], masks, preferred_element_type=f32).reshape(7, 49, 640)
-    pieces, index = [], 0
-    near = [n for n in range(343) if not tables()["pad"][n].astype(np.float32).any()]
-    position = 0
-    while position < 343:
-        stop = position
-        if position in near:
-            while stop in near:
-                stop += 1
-            pieces.append(jnp.zeros((stop - position, RANK, RANK), f32))
-        else:
-            while stop < 343 and stop not in near:
-                stop += 1
-            pieces.append(translations[index : index + stop - position])
-            index += stop - position
-        position = stop
-    operators = jnp.concatenate(pieces).reshape(49, 7, RANK, RANK)
-    operators = jnp.transpose(operators, (0, 2, 1, 3)).reshape(49, RANK, 7 * RANK)
-
     return pl.pallas_call(
         downward_kernel,
         out_shape=jax.ShapeDtypeStruct((RHS, points), f32),
         in_specs=[vmem] * 13,
         out_specs=vmem,
         scratch_shapes=[
+            pltpu.VMEM((30 * RANK, 192), bf16),
+            pltpu.VMEM((30 * RANK, 192), bf16),
             pltpu.VMEM((8, 7, 224, 128), bf16),
             pltpu.VMEM((8, 7, 224, 128), bf16),
             pltpu.VMEM((7, 7, 224, 128), bf16),
@@ -482,17 +616,17 @@
         ],
         compiler_params=params,
     )(
-        full,
+        exchanged,
         t["place"],
         t["target"],
-        operators,
+        translations,
         masks,
         t["back"],
         t["back_parent"],
         t["back_top"],
         expand,
         t["kron_t"],
-        coords,
+        point_coords,
         t["expander"],
         t["code"].reshape(512, 1),
     )

time: 123 us -> 78 us (0.63)
  local copies, waits for them, and re-layouts: 38.9 us -> 8.32 us
  Pallas kernels: 53.6 us -> 65.3 us
  starting transfers between devices: 11.5 us -> 0 us
  waiting for transfers between devices: 11.4 us -> 0 us
  other arithmetic: 4.76 us -> 2.2 us
    concatenate x3 -> x0, local copies, waits for them, and re-layouts: 12.8 us -> none  [the longest x2 12.8 us: body(): operators = jnp.concatenate(pieces).reshape(49, 7, RANK, RANK)]
    ppermute x4 -> x0, starting transfers between devices: 11.5 us -> none  [the longest x2 8.74 us: neighbours(): before = lax.ppermute(tail, axis, [(i, i + 1) for i in range(count - 1)])]
    ppermute x4 -> x0, waiting for transfers between devices: 11.4 us -> none  [the longest x2 7.28 us: neighbours(): before = lax.ppermute(tail, axis, [(i, i + 1) for i in range(count - 1)])]
    pallas_call x1 -> x2, Pallas kernels: 17.8 us -> 28.9 us  [the longest x1 17.9 us: body(): pl.pallas_call(upward_kernel, out_shape=jax.ShapeDtypeStruct((26, 16, 128...]
    slice x5 -> x0, local copies, waits for them, and re-layouts: 6.32 us -> none  [the longest x3 4.66 us: body(): pieces.append(translations[index:index + stop - position])]
    transpose x1 -> x0, local copies, waits for them, and re-layouts: 6 us -> none  [body(): jnp.transpose(operators, (0, 2, 1, 3)).reshape(49, RANK, 7 * RANK)]
    reshape x1 -> x0, local copies, waits for them, and re-layouts: 4.09 us -> none  [body(): jnp.transpose(operators, (0, 2, 1, 3)).reshape(49, RANK, 7 * RANK)]
    pad x2 -> x0, local copies, waits for them, and re-layouts: 3.02 us -> none  [the longest x1 1.52 us: body(): normals = jnp.pad(point_normals, ((0, 5), (0, 0)))]
  transfers between devices with their start and end apart: 4 -> 0, of which waited for: 2 -> 0; matrix products, arithmetic and copies ran while one was open for 28% -> 0% of each run, Pallas kernels for 0% -> 0%
where the time goes in v2:
time: 78 us; the launch traced here: 77.2 us
  Pallas kernels  65.3 us (84%)
  local copies, waits for them, and re-layouts  8.32 us (11%)
  other arithmetic  2.2 us (3%)
  matrix products  1.25 us (2%)
    pallas_call x1, Pallas kernels, body(): pl.pallas_call(downward_kernel, out_shape=jax.ShapeDtypeStruct((RHS, poin...  36.4 us
    pallas_call x1, Pallas kernels, body(): pl.pallas_call(upward_kernel, out_shape=jax.ShapeDtypeStruct((26, 16, 128...  17.9 us
    pallas_call x1, Pallas kernels, body(): pl.pallas_call(exchange_kernel, out_shape=jax.ShapeDtypeStruct((3, 26, 16...  11 us
    unnamed x18, local copies, waits for them, and re-layouts  7.1 us

profile of v2, /device:TPU:0, one launch (start us, length us, event | category | flops | bytes accessed | tf_op | source)
XLA Modules:
  0.0 77.2 jit_solution(4227478467295136498)
XLA Ops:
  0.0 0.0 copy-start.5
  0.0 0.0 copy-start.4
  0.0 0.8 %iota_compare_fusion = pred[256,16]{1,0:T(8,128)(4,1)S(1)} fusion(s32[256]{0:T(256)} %bitcast.11), kind=kLoop, calls=%fused_computation.10 | loop fusion | flops 4096 | bytes 5120 | tf_op jit(solution)/shard_map/lt | solution.py:552
  0.8 0.1 lt.26
  0.9 0.0 copy-start.6
  0.9 0.0 copy-start.7
  0.9 1.4 %broadcast_select_fusion.charges = f32[2,4096]{1,0:T(2,128)} fusion(f32[2,4096]{1,0:T(2,128)} %param.28, pred[4096]{0:T(1024)(128)(4,1)S(1)} %lt.26), kind=kLoop, calls=%fused_computation.11 | loop fusion | flops 8192 | bytes 69632 | tf_op jit(solution)/shard_map/jit(_where)/select_n | solution.py:553
  2.4 1.5 %copy.30.expand = f32[216,32]{1,0:T(8,128)} copy(f32[216,32]{0,1:T(8,128)} %param.35) | data formatting | bytes 55296 | tf_op args[9]
  3.9 0.0 copy-start.1
  3.9 0.0 copy-start.3
  3.9 0.0 copy-start.2
  3.9 17.9 %shard_map.244.coef = f32[26,16,128]{2,1,0:T(8,128)} custom-call(f32[3,4096]{1,0:T(4,128)} %coords.3, f32[3,4096]{1,0:T(4,128)} %normals.1, f32[2,4096]{1,0:T(2,128)} %broadcast_select_fusion.charges, bf16[648,144]{1,0:T(8,128)(2,1)} %constant.36.clone.expander, s32[1,512]{1,0:T(1,128)} %constant.37.clone.code, ...), custom_call_target="tpu_custom_call" | custom-call | tf_op jit(solution)/shard_map/pallas_call | solution.py:555
  21.8 0.0 copy-done.5
  21.8 0.0 copy-done.4
  21.8 0.2 fusion.8
  22.0 0.0 copy-done.6
  22.0 0.0 copy-done.7
  22.0 0.2 fusion.2
  22.3 0.0 copy-done.1
  22.3 0.0 copy-done.3
  22.3 0.3 fusion
  22.6 0.0 copy-done.2
  22.6 0.5 fusion.3
  23.1 0.0 copy-start
  23.1 1.1 %reshape.23.mask = f32[7,49,640]{2,1,0:T(8,128)} reshape(f32[343,640]{1,0:T(8,128)S(1)} %fusion.3) | data formatting | bytes 1756160 | tf_op jit(solution)/shard_map/reshape | solution.py:598
  24.2 11.0 %shard_map.245.exchanged = f32[3,26,16,128]{3,2,1,0:T(8,128)} custom-call(f32[26,16,128]{2,1,0:T(8,128)} %shard_map.244.coef), custom_call_target="tpu_custom_call" | custom-call | tf_op jit(solution)/shard_map/pallas_call | solution.py:575
  35.2 0.0 copy-done
  35.2 5.6 %copy.29.translations = f32[316,32,32]{2,1,0:T(8,128)} copy(f32[316,32,32]{0,2,1:T(8,128)S(1)} %copy-done) | data formatting | bytes 2588672 | tf_op args[7]
  40.8 36.4 %shard_map.246 = f32[2,4096]{1,0:T(2,128)} custom-call(f32[3,26,16,128]{3,2,1,0:T(8,128)} %shard_map.245.exchanged, bf16[8,192,256]{2,1,0:T(8,128)(2,1)} %constant.42.clone.place, s32[2,7,7,128]{3,2,1,0:T(8,128)} %constant.38.clone.target, f32[316,32,32]{2,1,0:T(8,128)} %copy.29.translations, f32[7,49,640]{2,1,0:T(8,128)} %reshape.23.mask, ...), custom_call_target="tpu_custom_call" | custom-call | tf_op jit(solution)/shard_map/pallas_call | solution.py:599
Async XLA Ops:
  0.0 21.8 %copy-start.5 = (bf16[32,128]{1,0:T(8,128)(2,1)S(1)}, bf16[32,128]{1,0:T(8,128)(2,1)}, u32[]{:S(2)}) copy-start(bf16[32,128]{1,0:T(8,128)(2,1)} %constant.47.clone) | copy-start | bytes 24580
  0.0 21.8 %copy-start.4 = (s32[32,316]{1,0:T(8,128)S(1)}, s32[32,316]{1,0:T(8,128)}, u32[]{:S(2)}) copy-start(s32[32,316]{1,0:T(8,128)} %param.31) | copy-start | bytes 121348
  0.9 21.1 %copy-start.6 = (s32[4,316]{1,0:T(4,128)S(1)}, s32[4,316]{1,0:T(4,128)}, u32[]{:S(2)}) copy-start(s32[4,316]{1,0:T(4,128)} %param.32) | copy-start | bytes 15172
  0.9 21.1 %copy-start.7 = (bf16[4,128]{1,0:T(4,128)(2,1)S(1)}, bf16[4,128]{1,0:T(4,128)(2,1)}, u32[]{:S(2)}) copy-start(bf16[4,128]{1,0:T(4,128)(2,1)} %constant.48.clone) | copy-start | bytes 3076
  3.9 18.4 %copy-start.1 = (s32[256,316]{0,1:T(8,128)S(1)}, s32[256,316]{0,1:T(8,128)}, u32[]{:S(2)}) copy-start(s32[256,316]{0,1:T(8,128)} %param.30) | copy-start | bytes 970756
  3.9 18.4 %copy-start.3 = (bf16[256,512]{1,0:T(8,128)(2,1)S(1)}, bf16[256,512]{1,0:T(8,128)(2,1)}, u32[]{:S(2)}) copy-start(bf16[256,512]{1,0:T(8,128)(2,1)} %constant.46.clone) | copy-start | bytes 786436
  3.9 18.8 %copy-start.2 = (bf16[343,316]{1,0:T(8,128)(2,1)S(1)}, bf16[343,316]{1,0:T(8,128)(2,1)}, u32[]{:S(2)}) copy-start(bf16[343,316]{1,0:T(8,128)(2,1)} %constant.49.clone) | copy-start | bytes 650332
  23.1 12.1 %copy-start = (f32[316,32,32]{0,2,1:T(8,128)S(1)}, f32[316,32,32]{0,2,1:T(8,128)}, u32[]{:S(2)}) copy-start(f32[316,32,32]{0,2,1:T(8,128)} %param.33) | copy-start | bytes 3883012
